TPU v7x, 512 devices: a whole 4x8x8 slice. The times are simulated.
512 devices in a mesh: aa: 8 (over z), ba: 16 (over y, core), col: 4 (over x).
Axes of the slice: x: 4, y: 8, z: 8, core: 2. Of those that a mesh axis runs over, the one named last changes fastest.
Arguments:
- tensor: bfloat16 [512, 512, 512], P('aa', 'ba', 'col'), may hold values from -24 to 24
- factor_b_init: float32 [512, 256], P(('ba', 'aa', 'col')), may hold values from -5.2 to 6.8
- factor_c_init: float32 [512, 256], P(('col', 'aa', 'ba')), may hold values from -5.2 to 6.8
Outputs:
- factor_a: float32 [512, 256], P(('aa', 'ba', 'col'))
- factor_b: float32 [512, 256], P(('ba', 'aa', 'col'))
- factor_c: float32 [512, 256], P(('col', 'aa', 'ba'))
All inputs are finite; a program needn't handle non-finite values.
Results may differ from a plain program's by a relative error of at most 0.007.
The roundings to bfloat16 on the way count: a program that leaves them out, or rounds other values in their place, can miss the bound.
Values may be sent and summed in bfloat16 or wider, within the bound.
No kernel may reach another device: no remote copies, remote signals or barrier semaphores. Data moves between devices by JAX's collectives and lax.ppermute only.
A program may use at most 64 MiB of HBM per device.

v0:
```python
import functools

import jax
import jax.numpy as jnp
from jax import lax
from jax.experimental import pallas as pl
from jax.experimental.pallas import tpu as pltpu
from jax.sharding import Mesh, PartitionSpec as P

EPSILON = 1e-06
HIGHEST = lax.Precision.HIGHEST
F32 = jnp.float32


def dot(left, right):
    return jnp.dot(left, right, precision=HIGHEST, preferred_element_type=F32)


def gram_of(rows):
    return lax.dot_general(rows, rows, (((0,), (0,)), ((), ())), precision=HIGHEST, preferred_element_type=F32)


SUB = 8
PANEL = 128
N_COL = 4


def tree_sum(terms):
    while len(terms) > 1:
        terms = [terms[n] + terms[n + 1] if n + 1 < len(terms) else terms[n] for n in range(0, len(terms), 2)]
    return terms[0]


def invert_tile(columns, row_id):
    for k in range(0, SUB, 2):
        a, b = columns[k][k : k + 1, :], columns[k + 1][k : k + 1, :]
        c, d = columns[k][k + 1 : k + 2, :], columns[k + 1][k + 1 : k + 2, :]
        inv = 1.0 / (a * d - b * c)
        first = (d * inv, -b * inv)
        second = (-c * inv, a * inv)
        inside = (row_id == k) | (row_id == k + 1)
        left = jnp.where(row_id == k, -1.0, jnp.where(row_id == k + 1, 0.0, columns[k]))
        right = jnp.where(row_id == k + 1, -1.0, jnp.where(row_id == k, 0.0, columns[k + 1]))
        updated = []
        for j in range(SUB):
            if j in (k, k + 1):
                top, low, base = first[j - k], second[j - k], 0.0
            else:
                x, y = columns[j][k : k + 1, :], columns[j][k + 1 : k + 2, :]
                top, low = first[0] * x + first[1] * y, second[0] * x + second[1] * y
                base = jnp.where(inside, 0.0, columns[j])
            updated.append(base - (left * top + right * low))
        columns = updated
    return columns


def invert_panel(matrix):
    size = matrix.shape[0]
    row_id = lax.broadcasted_iota(jnp.int32, (SUB, size), 0)
    col_id = lax.broadcasted_iota(jnp.int32, (SUB, size), 1)
    tiles = [matrix[lo : lo + SUB, :] for lo in range(0, size, SUB)]
    plain, scaled = [], []
    for q in range(size // SUB):
        lo = q * SUB
        columns = [jnp.broadcast_to(tiles[q][:, lo + j : lo + j + 1], (SUB, size)) for j in range(SUB)]
        columns = invert_tile(columns, row_id)
        inside = (col_id >= lo) & (col_id < lo + SUB)
        pivot = jnp.where(inside, jnp.where(col_id - lo == row_id, 1.0, 0.0), tiles[q])
        rows = tree_sum([columns[j] * pivot[j : j + 1, :] for j in range(SUB)])
        known = col_id < lo + SUB
        plain.append(jnp.where(known, pivot, 0.0))
        scaled.append(jnp.where(known, rows, 0.0))
        for i in range(q + 1, size // SUB):
            tile = tiles[i]
            terms = [tile[:, lo + j : lo + j + 1] * rows[j : j + 1, :] for j in range(SUB)]
            tiles[i] = jnp.where(inside, 0.0, tile) - tree_sum(terms)
    return lax.dot_general(
        jnp.concatenate(plain, axis=0),
        jnp.concatenate(scaled, axis=0),
        (((0,), (0,)), ((), ())),
        precision=HIGHEST,
        preferred_element_type=F32,
    )


def invert_into(matrix, out_ref):
    head = matrix[:PANEL, :PANEL]
    cross = matrix[:PANEL, PANEL:]
    head_inverse = invert_panel(head)
    solved = dot(head_inverse, cross)
    tail_inverse = invert_panel(matrix[PANEL:, PANEL:] - dot(matrix[PANEL:, :PANEL], solved))
    mixed = dot(solved, tail_inverse)
    out_ref[PANEL:, PANEL:] = tail_inverse
    out_ref[:PANEL, PANEL:] = -mixed
    out_ref[PANEL:, :PANEL] = -mixed.T
    out_ref[:PANEL, :PANEL] = head_inverse + lax.dot_general(
        mixed, solved, (((1,), (1,)), ((), ())), precision=HIGHEST, preferred_element_type=F32
    )


ROWS = 8


def one_hot(shape, wanted):
    return jnp.where(lax.broadcasted_iota(jnp.int32, shape, 1) == wanted, 1.0, 0.0)


def first_kernel(place_ref, tensor_ref, own_ref, other_ref, c_block_ref, out_ref):
    y, core, col = place_ref[1], place_ref[2], place_ref[3]
    blk_i, blk_j, blk_k = tensor_ref.shape
    plane, rank = own_ref.shape[0], c_block_ref.shape[1]
    n_col = N_COL
    k = lax.broadcasted_iota(jnp.int32, (blk_k, plane), 0)
    at = k // 16 * (8 * n_col) + k % 16 // 2 * n_col + col
    c_low_own = own_ref[:, rank:].astype(jnp.bfloat16)
    c_low_other = other_ref[:, rank:].astype(jnp.bfloat16)
    mine = k % 2 == core
    pick_own = one_hot((blk_k, plane), jnp.where(mine, at, -1)).astype(jnp.bfloat16)
    pick_other = one_hot((blk_k, plane), jnp.where(mine, -1, at)).astype(jnp.bfloat16)
    c_block = jnp.dot(pick_own, c_low_own, preferred_element_type=F32) + jnp.dot(
        pick_other, c_low_other, preferred_element_type=F32
    )
    c_block = c_block.astype(jnp.bfloat16)
    c_block_ref[...] = c_block
    j = lax.broadcasted_iota(jnp.int32, (blk_j, plane), 0)
    b_block = dot(one_hot((blk_j, plane), j // n_col * (8 * n_col) + y * n_col + j % n_col), own_ref[:, :rank])
    for lo in range(0, blk_i, ROWS):
        flat = tensor_ref[lo : lo + ROWS].reshape(ROWS * blk_j, blk_k)
        inner = jnp.dot(flat, c_block, preferred_element_type=F32)
        for i in range(lo, lo + ROWS):
            row = jnp.sum(inner[(i - lo) * blk_j : (i - lo + 1) * blk_j] * b_block, axis=0, keepdims=True)
            for copy in range(n_col):
                out_ref[i // n_col * n_col + copy, i % n_col : i % n_col + 1, :] = row


def second_kernel(place_ref, tensor_ref, c_block_ref, own_ref, other_ref, solve_ref, raw_ref, row_ref, out_ref):
    aa, y, core, col = place_ref[0], place_ref[1], place_ref[2], place_ref[3]
    blk_i, blk_j, blk_k = tensor_ref.shape
    half = blk_i // 2
    n_col = N_COL
    lo = pl.multiple_of(aa * half, half)
    raw_own = dot(own_ref[pl.ds(lo, half), :], solve_ref[...])
    raw_other = dot(other_ref[pl.ds(lo, half), :], solve_ref[...])
    even = jnp.where(core == 0, raw_own, raw_other)
    odd = jnp.where(core == 0, raw_other, raw_own)
    for step in range(half // n_col):
        raw_ref[2 * step * n_col : (2 * step + 1) * n_col, :] = even[step * n_col : (step + 1) * n_col]
        raw_ref[(2 * step + 1) * n_col : (2 * step + 2) * n_col, :] = odd[step * n_col : (step + 1) * n_col]
    row_ref[...] = raw_ref[pl.ds((2 * y + core) * n_col + col, 1), :]
    c_block = c_block_ref[...]
    total = jnp.zeros((blk_j, row_ref.shape[1]), F32)
    for lo in range(0, blk_i, ROWS):
        flat = tensor_ref[lo : lo + ROWS].reshape(ROWS * blk_j, blk_k)
        inner = jnp.dot(flat, c_block, preferred_element_type=F32)
        for i in range(ROWS):
            total = total + inner[i * blk_j : (i + 1) * blk_j] * raw_ref[lo + i : lo + i + 1, :]
    rows = out_ref.shape[1]
    for dest in range(out_ref.shape[0]):
        lo = dest % n_col * blk_j // n_col // rows * rows
        out_ref[dest] = total[lo : lo + rows]


def given_kernel(own_ref, other_ref, _, inverse_ref, gram_c_ref):
    rank = inverse_ref.shape[0]
    gram_b = gram_of(own_ref[:, :rank]) + gram_of(other_ref[:, :rank])
    gram_c = gram_of(own_ref[:, rank:]) + gram_of(other_ref[:, rank:])
    gram_c_ref[...] = gram_c
    invert_into(gram_b * gram_c, inverse_ref)


def scaled_kernel(
    own_ref, other_ref, solve_ref, other_gram_ref, block_ref, row_ref, _, next_ref, gram_ref, low_ref, out_row_ref
):
    gram = gram_of(dot(own_ref[...], solve_ref[...])) + gram_of(dot(other_ref[...], solve_ref[...]))
    size = gram.shape[0]
    total_rows = 2 * own_ref.shape[0]
    row_id = lax.broadcasted_iota(jnp.int32, (size, size), 0)
    col_id = lax.broadcasted_iota(jnp.int32, (size, size), 1)
    squares = jnp.where(row_id == col_id, gram, 0.0)
    by_col = 1.0 / jnp.sqrt(jnp.sum(squares, axis=0, keepdims=True) / total_rows + EPSILON)
    by_row = 1.0 / jnp.sqrt(jnp.sum(squares, axis=1, keepdims=True) / total_rows + EPSILON)
    gram = gram * by_row * by_col
    low_ref[...] = (block_ref[...] * by_col).astype(low_ref.dtype)
    out_row_ref[...] = row_ref[...] * by_col
    gram_ref[...] = gram
    invert_into(gram * other_gram_ref[...], next_ref)
    next_ref[...] = next_ref[...] * by_row


def given_copies_kernel(b_ref, c_ref, out_ref):
    row = jnp.concatenate([b_ref[...], c_ref[...]], axis=1)
    out_ref[...] = jnp.broadcast_to(row[None], out_ref.shape)


def spread_kernel(parts_ref, *refs):
    out_ref = refs[-1]
    total = jnp.sum(parts_ref[...], axis=0)
    out_ref[...] = jnp.broadcast_to(total[None], out_ref.shape)


def apply_kernel(parts_ref, solve_ref, raw_ref, squares_ref):
    raw = dot(jnp.sum(parts_ref[...], axis=0), solve_ref[...])
    raw_ref[...] = raw
    squares_ref[...] = jnp.broadcast_to((raw * raw)[None], squares_ref.shape)


def scale_kernel(total_rows, parts_ref, raw_ref, out_ref):
    squares = jnp.sum(parts_ref[...], axis=0)
    out_ref[...] = raw_ref[...] / jnp.sqrt(squares / total_rows + EPSILON)


def local_call(kernel, out_shapes, *operands, flops=10**6, waits=0, place=None):
    vmem = pl.BlockSpec(memory_space=pltpu.VMEM)
    specs = [vmem] * (len(operands) - waits) + [pl.BlockSpec(memory_space=pl.ANY)] * waits
    if place is not None:
        operands, specs = (place,) + operands, [pl.BlockSpec(memory_space=pltpu.SMEM)] + specs
    return pl.pallas_call(
        kernel,
        out_shape=[s if isinstance(s, jax.ShapeDtypeStruct) else jax.ShapeDtypeStruct(s, F32) for s in out_shapes],
        in_specs=specs,
        out_specs=[vmem] * len(out_shapes),
        compiler_params=pltpu.CompilerParams(vmem_limit_bytes=24 * 2**20),
        cost_estimate=pl.CostEstimate(flops=flops, bytes_accessed=2**20, transcendentals=0),
    )(*operands)


def axes_size(axes):
    size = 1
    for axis in axes:
        size *= lax.axis_size(axis)
    return size


def exchange(blocks, axes):
    return lax.all_to_all(blocks, axes, 0, 0, tiled=True)


COL = ("col_hi", "col_lo")
PLANE = ("aa", "y") + COL


def gather_all(copies, axes):
    own = exchange(copies, axes).reshape(copies.shape[0] * copies.shape[1], copies.shape[2])
    return own, lax.ppermute(own, "core", [(0, 1), (1, 0)])


def body(tensor, b_row, c_row):
    blk_i, blk_j, blk_k = tensor.shape
    rank = b_row.shape[1]
    n_aa, n_y, n_core, n_hi = (lax.axis_size(axis) for axis in ("aa", "y", "core", "col_hi"))
    n_col = axes_size(COL)
    aa, y, core, col = (lax.axis_index(axis) for axis in ("aa", "y", "core", COL))
    place = jnp.stack([aa, y, core, col]).astype(jnp.int32)
    square, heavy = (rank, rank), 12 * 10**9
    planes = axes_size(PLANE)
    a_parts = (n_aa * n_y, blk_i // (n_y * n_core), rank)
    b_parts = (n_y * n_hi, blk_j // n_hi, rank)
    low = lambda rows: jax.ShapeDtypeStruct((rows, rank), jnp.bfloat16)

    copies = local_call(given_copies_kernel, [(planes, 1, 2 * rank)], b_row, c_row)[0]
    own, other = gather_all(copies, PLANE)
    c_block, partial = local_call(
        first_kernel, [low(blk_k), (n_y * n_core * n_col,) + a_parts[1:]], tensor, own, other, flops=4 * 10**9, place=place
    )
    parts = exchange(partial, ("y", "core") + COL)
    solve, gram_c = local_call(given_kernel, [square, square], own, other, partial, flops=heavy, waits=1)
    own, other = gather_all(local_call(spread_kernel, [a_parts], parts, solve, waits=1)[0], ("aa", "y"))

    raw_a, row, partial = local_call(
        second_kernel,
        [(blk_i, rank), (1, rank), (n_aa * n_col,) + b_parts[1:]],
        tensor, c_block, own, other, solve,
        flops=4 * 10**9, place=place,
    )
    parts = exchange(partial, ("aa",) + COL)
    solve, gram_a, a_low, factor_a = local_call(
        scaled_kernel,
        [square, square, low(blk_i), (1, rank)],
        own, other, solve, gram_c, raw_a, row, partial,
        flops=heavy, waits=1,
    )
    own, other = gather_all(local_call(spread_kernel, [b_parts], parts, solve, waits=1)[0], ("y", "col_hi"))
    raw_b = dot(lax.dynamic_slice_in_dim(own, y * blk_j, blk_j, 0), solve)

    inner = jnp.einsum("ijk,ir->jkr", tensor, a_low, preferred_element_type=F32)
    partial = jnp.sum(inner * raw_b[:, None], axis=0).reshape(blk_k, 1, rank)
    parts = exchange(partial, ("aa", "y", "core"))
    row = lax.dynamic_slice_in_dim(raw_b, aa * n_col + col, 1, 0)
    solve, _, _, factor_b = local_call(
        scaled_kernel,
        [square, square, low(blk_j), (1, rank)],
        own, other, solve, gram_a, raw_b, row, partial,
        flops=heavy, waits=1,
    )

    near, far = ("aa", "core"), ("y",) + COL
    raw_c, squares = local_call(apply_kernel, [(1, rank), (axes_size(near), 1, rank)], parts, solve)
    squares = local_call(spread_kernel, [(axes_size(far), 1, rank)], exchange(squares, near))[0]
    scale = functools.partial(scale_kernel, blk_k * n_col)
    factor_c = local_call(scale, [(1, rank)], exchange(squares, far), raw_c)[0]
    return factor_a, factor_b, factor_c


def solution(mesh):
    n_aa, n_ba, n_col = mesh.devices.shape
    fine = Mesh(
        mesh.devices.reshape(n_aa, n_ba // 2, 2, n_col // 2, 2), ("aa", "y", "core", "col_hi", "col_lo")
    )
    a_spec = P(("aa", "y", "core") + COL, None)
    b_spec = P(("y", "core", "aa") + COL, None)
    c_spec = P(COL + ("aa", "y", "core"), None)
    return jax.shard_map(
        body,
        mesh=fine,
        in_specs=(P("aa", ("y", "core"), COL), b_spec, c_spec),
        out_specs=(a_spec, b_spec, c_spec),
        check_vma=False,
    )
```

profile of v0, /device:TPU:1, one launch (start us, length us, event | category | flops | bytes accessed | tf_op | source)
XLA Modules:
  0.0 187.7 jit_solution(784170647729565158)
XLA Ops:
  0.6 0.0 copy-start
  0.6 0.7 copy-done
  1.3 0.0 copy-start.1
  1.3 0.7 copy-done.1
  2.0 0.1 shard_map.58
  2.1 40.5 %all_to_all.40 = f32[256,1,512]{2,1,0:T(1,128)S(1)} all-to-all(f32[256,1,512]{2,1,0:T(1,128)S(1)} %shard_map.58), channel_id=1, replica_groups=mesh['aa'=8,'y'=8,'core'=2,'col_hi'=2,'col_lo'=2] {'aa','y','col_hi','co..., dimensions={0} | all-to-all | bytes 1048576 | tf_op jit(solution)/shard_map/all_to_all | solution.py:235
  42.6 0.0 copy-start.2
  42.6 5.2 %collective-permute-start = (f32[256,512]{1,0:T(8,128)S(1)}, f32[256,512]{1,0:T(8,128)S(1)}, u32[]{:S(2)}, u32[]{:S(2)}) collective-permute-start(f32[256,512]{1,0:T(8,128)S(1)} %bitcast.17), channel_id=1, source_target_pairs={{0,4},{4,0},{1,5},{5,1},{2,6},{6,2},{3,7},{7,3},{8,12},{12,8},{9,1... | collective-permute-start | bytes 1572872 | tf_op jit(solution)/shard_map/ppermute | solution.py:244
  47.9 0.1 pad_add_fusion.place_ref
  48.0 1.4 collective-permute-done.other_ref
  49.4 0.0 copy-done.2
  49.4 2.0 %shard_map.59 = (bf16[128,256]{1,0:T(8,128)(2,1)S(1)}, f32[64,4,256]{2,1,0:T(4,128)}) custom-call(s32[4]{0:T(128)S(1)} %pad_add_fusion.place_ref, bf16[64,32,128]{2,1,0:T(8,128)(2,1)S(1)} %copy-done.2, f32[256,512]{1,0:T(8,128)S(1)} %bitcast.18, f32[256,512]{1,0:T(8,128)S(1)} %collective-permute-done.other_ref), custom_call_target="tpu_custom_call" | custom-call | flops 4000000000 | bytes 1048576 | tf_op jit(solution)/shard_map/pallas_call | solution.py:217
  51.4 5.5 %all-to-all-start.1 = ((f32[64,4,256]{2,1,0:T(4,128)}), f32[64,4,256]{2,1,0:T(4,128)S(1)}, u32[]{:S(2)}, u32[]{:S(2)}) async-start(f32[64,4,256]{2,1,0:T(4,128)} %get-tuple-element.18._), calls=%async_computation.1 | async-start | bytes 524288 | tf_op jit(solution)/shard_map/all_to_all | solution.py:235
  56.9 9.1 %shard_map.60 = (f32[256,256]{1,0:T(8,128)S(1)}, f32[256,256]{1,0:T(8,128)S(1)}) custom-call(f32[256,512]{1,0:T(8,128)S(1)} %bitcast.19, f32[256,512]{1,0:T(8,128)S(1)} %collective-permute-done.other_ref, f32[64,4,256]{2,1,0:T(4,128)} %get-tuple-element.18._), custom_call_target="tpu_custom_call" | custom-call | flops 12000000000 | bytes 1048576 | tf_op jit(solution)/shard_map/pallas_call | solution.py:217
  66.1 3.1 %all-to-all-done.1.parts_ref = f32[64,4,256]{2,1,0:T(4,128)S(1)} async-done(((f32[64,4,256]{2,1,0:T(4,128)}), f32[64,4,256]{2,1,0:T(4,128)S(1)}, u32[]{:S(2)}, u32[]{:S(2)}) %all-to-all-start.1) | async-done | bytes 262176 | tf_op jit(solution)/shard_map/all_to_all | solution.py:235
  69.2 0.1 shard_map.61
  69.3 18.1 %all_to_all.41 = f32[64,4,256]{2,1,0:T(4,128)S(1)} all-to-all(f32[64,4,256]{2,1,0:T(4,128)S(1)} %shard_map.61), channel_id=1, replica_groups=mesh['aa'=8,'y'=8,'core'=2,'col_hi'=2,'col_lo'=2] {'aa','y'}, dimensions={0} | all-to-all | bytes 524288 | tf_op jit(solution)/shard_map/all_to_all | solution.py:235
  87.4 0.1 reshape.20.own_ref
  87.5 4.9 %collective-permute-start.1 = (f32[256,256]{1,0:T(8,128)S(1)}, f32[256,256]{1,0:T(8,128)S(1)}, u32[]{:S(2)}, u32[]{:S(2)}) collective-permute-start(f32[256,256]{1,0:T(8,128)S(1)} %reshape.20.own_ref), channel_id=1, source_target_pairs={{0,4},{4,0},{1,5},{5,1},{2,6},{6,2},{3,7},{7,3},{8,12},{12,8},{9,1... | collective-permute-start | bytes 786440 | tf_op jit(solution)/shard_map/ppermute | solution.py:244
  92.4 1.1 collective-permute-done.1.other_ref
  93.5 2.1 %shard_map.62 = (f32[64,256]{1,0:T(8,128)S(1)}, f32[1,256]{1,0:T(1,128)S(1)}, f32[32,16,256]{2,1,0:T(8,128)}) custom-call(s32[4]{0:T(128)S(1)} %pad_add_fusion.place_ref, bf16[64,32,128]{2,1,0:T(8,128)(2,1)S(1)} %copy-done.2, bf16[128,256]{1,0:T(8,128)(2,1)S(1)} %get-tuple-element.21.c_block_ref, f32[256,256]{1,0:T(8,128)S(1)} %reshape.20.own_ref, ...), custom_call_target="tpu_custom_call" | custom-call | flops 4000000000 | bytes 1048576 | tf_op jit(solution)/shard_map/pallas_call | solution.py:217
  95.6 5.6 %all-to-all-start.3 = ((f32[32,16,256]{2,1,0:T(8,128)}), f32[32,16,256]{2,1,0:T(8,128)S(1)}, u32[]{:S(2)}, u32[]{:S(2)}) async-start(f32[32,16,256]{2,1,0:T(8,128)} %get-tuple-element.24._), calls=%async_computation.3 | async-start | bytes 1048576 | tf_op jit(solution)/shard_map/all_to_all | solution.py:235
  101.2 9.7 %shard_map.63 = (f32[256,256]{1,0:T(8,128)S(1)}, f32[256,256]{1,0:T(8,128)S(1)}, bf16[64,256]{1,0:T(8,128)(2,1)S(1)}, f32[1,256]{1,0:T(1,128)}) custom-call(f32[256,256]{1,0:T(8,128)S(1)} %reshape.20.own_ref, f32[256,256]{1,0:T(8,128)S(1)} %collective-permute-done.1.other_ref, f32[256,256]{1,0:T(8,128)S(1)} %get-tuple-element.19.refs_0_.solve_ref, ...), custom_call_target="tpu_custom_call" | custom-call | flops 12000000000 | bytes 1048576 | tf_op jit(solution)/shard_map/pallas_call | solution.py:217
  110.9 6.6 %all-to-all-done.3.parts_ref = f32[32,16,256]{2,1,0:T(8,128)S(1)} async-done(((f32[32,16,256]{2,1,0:T(8,128)}), f32[32,16,256]{2,1,0:T(8,128)S(1)}, u32[]{:S(2)}, u32[]{:S(2)}) %all-to-all-start.3) | async-done | bytes 524320 | tf_op jit(solution)/shard_map/all_to_all | solution.py:235
  117.5 0.8 shard_map.64
  118.3 3.9 %all-to-all-start.4 = ((f32[16,16,256]{2,1,0:T(8,128)}), f32[16,16,256]{2,1,0:T(8,128)S(1)}, u32[]{:S(2)}, u32[]{:S(2)}) async-start(f32[16,16,256]{2,1,0:T(8,128)} %shard_map.64), calls=%async_computation.4 | async-start | bytes 524288 | tf_op jit(solution)/shard_map/all_to_all | solution.py:235
  122.2 11.1 %all-to-all-done.4 = f32[16,16,256]{2,1,0:T(8,128)S(1)} async-done(((f32[16,16,256]{2,1,0:T(8,128)}), f32[16,16,256]{2,1,0:T(8,128)S(1)}, u32[]{:S(2)}, u32[]{:S(2)}) %all-to-all-start.4) | async-done | bytes 262176 | tf_op jit(solution)/shard_map/all_to_all | solution.py:235
  133.3 5.5 %collective-permute-start.2 = (f32[256,256]{1,0:T(8,128)S(1)}, f32[256,256]{1,0:T(8,128)S(1)}, u32[]{:S(2)}, u32[]{:S(2)}) collective-permute-start(f32[256,256]{1,0:T(8,128)S(1)} %bitcast.20), channel_id=1, source_target_pairs={{0,4},{4,0},{1,5},{5,1},{2,6},{6,2},{3,7},{7,3},{8,12},{12,8},{9,1... | collective-permute-start | bytes 786440 | tf_op jit(solution)/shard_map/ppermute | solution.py:244
  138.8 0.2 fusion.6.block_ref
  139.0 1.5 fusion
  140.6 0.8 copy.10._
  141.4 5.6 %all-to-all-start.5 = ((f32[128,1,256]{2,1,0:T(1,128)}), f32[128,1,256]{2,1,0:T(1,128)S(1)}, u32[]{:S(2)}, u32[]{:S(2)}) async-start(f32[128,1,256]{2,1,0:T(1,128)} %copy.10._), calls=%async_computation.5 | async-start | bytes 262144 | tf_op jit(solution)/shard_map/all_to_all | solution.py:235
  147.0 0.0 collective-permute-done.2.other_ref
  147.0 9.7 %shard_map.65 = (f32[256,256]{1,0:T(8,128)S(1)}, f32[256,256]{1,0:T(8,128)}, bf16[32,256]{1,0:T(8,128)(2,1)}, f32[1,256]{1,0:T(1,128)}) custom-call(f32[256,256]{1,0:T(8,128)S(1)} %bitcast.22, f32[256,256]{1,0:T(8,128)S(1)} %collective-permute-done.2.other_ref, f32[256,256]{1,0:T(8,128)S(1)} %get-tuple-element.26.refs_0_.solve_ref, ...), custom_call_target="tpu_custom_call" | custom-call | flops 12000000000 | bytes 1048576 | tf_op jit(solution)/shard_map/pallas_call | solution.py:217
  156.7 3.0 %all-to-all-done.5.parts_ref = f32[128,1,256]{2,1,0:T(1,128)S(1)} async-done(((f32[128,1,256]{2,1,0:T(1,128)}), f32[128,1,256]{2,1,0:T(1,128)S(1)}, u32[]{:S(2)}, u32[]{:S(2)}) %all-to-all-start.5) | async-done | bytes 131104 | tf_op jit(solution)/shard_map/all_to_all | solution.py:235
  159.7 0.4 shard_map.66
  160.1 11.7 %all_to_all.42.parts_ref = f32[16,1,256]{2,1,0:T(1,128)S(1)} all-to-all(f32[16,1,256]{2,1,0:T(1,128)S(1)} %get-tuple-element.31), channel_id=1, replica_groups=mesh['aa'=8,'y'=8,'core'=2,'col_hi'=2,'col_lo'=2] {'aa','core'}, dimensions={0} | all-to-all | bytes 32768 | tf_op jit(solution)/shard_map/all_to_all | solution.py:235
  171.8 15.3 %all_to_all.43.parts_ref = f32[32,1,256]{2,1,0:T(1,128)S(1)} all-to-all(f32[32,1,256]{2,1,0:T(1,128)S(1)} %shard_map.67), channel_id=1, replica_groups=mesh['aa'=8,'y'=8,'core'=2,'col_hi'=2,'col_lo'=2] {'y','col_hi','col_lo'}, dimensions={0} | all-to-all | bytes 65536 | tf_op jit(solution)/shard_map/all_to_all | solution.py:235
  187.1 0.6 shard_map.68
  (3 shorter events, 0.1 us)
Async XLA Ops:
  0.6 0.7 copy-start
  1.3 0.7 copy-start.1
  42.6 6.8 %copy-start.2 = (bf16[64,32,128]{2,1,0:T(8,128)(2,1)S(1)}, bf16[64,32,128]{2,1,0:T(8,128)(2,1)}, u32[]{:S(2)}) copy-start(bf16[64,32,128]{2,1,0:T(8,128)(2,1)} %tensor_ref.3) | copy-start | bytes 1572868
  42.6 6.8 %collective-permute-start = (f32[256,512]{1,0:T(8,128)S(1)}, f32[256,512]{1,0:T(8,128)S(1)}, u32[]{:S(2)}, u32[]{:S(2)}) collective-permute-start(f32[256,512]{1,0:T(8,128)S(1)} %bitcast.17), channel_id=1, source_target_pairs={{0,4},{4,0},{1,5},{5,1},{2,6},{6,2},{3,7},{7,3},{8,12},{12,8},{9,1... | collective-permute-start | bytes 1572872 | tf_op jit(solution)/shard_map/ppermute | solution.py:244
  51.4 17.8 %all-to-all-start.1 = ((f32[64,4,256]{2,1,0:T(4,128)}), f32[64,4,256]{2,1,0:T(4,128)S(1)}, u32[]{:S(2)}, u32[]{:S(2)}) async-start(f32[64,4,256]{2,1,0:T(4,128)} %get-tuple-element.18._), calls=%async_computation.1 | async-start | bytes 524288 | tf_op jit(solution)/shard_map/all_to_all | solution.py:235
  87.5 6.0 %collective-permute-start.1 = (f32[256,256]{1,0:T(8,128)S(1)}, f32[256,256]{1,0:T(8,128)S(1)}, u32[]{:S(2)}, u32[]{:S(2)}) collective-permute-start(f32[256,256]{1,0:T(8,128)S(1)} %reshape.20.own_ref), channel_id=1, source_target_pairs={{0,4},{4,0},{1,5},{5,1},{2,6},{6,2},{3,7},{7,3},{8,12},{12,8},{9,1... | collective-permute-start | bytes 786440 | tf_op jit(solution)/shard_map/ppermute | solution.py:244
  95.6 21.9 %all-to-all-start.3 = ((f32[32,16,256]{2,1,0:T(8,128)}), f32[32,16,256]{2,1,0:T(8,128)S(1)}, u32[]{:S(2)}, u32[]{:S(2)}) async-start(f32[32,16,256]{2,1,0:T(8,128)} %get-tuple-element.24._), calls=%async_computation.3 | async-start | bytes 1048576 | tf_op jit(solution)/shard_map/all_to_all | solution.py:235
  118.3 15.0 %all-to-all-start.4 = ((f32[16,16,256]{2,1,0:T(8,128)}), f32[16,16,256]{2,1,0:T(8,128)S(1)}, u32[]{:S(2)}, u32[]{:S(2)}) async-start(f32[16,16,256]{2,1,0:T(8,128)} %shard_map.64), calls=%async_computation.4 | async-start | bytes 524288 | tf_op jit(solution)/shard_map/all_to_all | solution.py:235
  133.3 13.7 %collective-permute-start.2 = (f32[256,256]{1,0:T(8,128)S(1)}, f32[256,256]{1,0:T(8,128)S(1)}, u32[]{:S(2)}, u32[]{:S(2)}) collective-permute-start(f32[256,256]{1,0:T(8,128)S(1)} %bitcast.20), channel_id=1, source_target_pairs={{0,4},{4,0},{1,5},{5,1},{2,6},{6,2},{3,7},{7,3},{8,12},{12,8},{9,1... | collective-permute-start | bytes 786440 | tf_op jit(solution)/shard_map/ppermute | solution.py:244
  141.4 18.4 %all-to-all-start.5 = ((f32[128,1,256]{2,1,0:T(1,128)}), f32[128,1,256]{2,1,0:T(1,128)S(1)}, u32[]{:S(2)}, u32[]{:S(2)}) async-start(f32[128,1,256]{2,1,0:T(1,128)} %copy.10._), calls=%async_computation.5 | async-start | bytes 262144 | tf_op jit(solution)/shard_map/all_to_all | solution.py:235
where the time goes:
time: 188 us
  blocking collectives  85.6 us (46%)
  starting transfers between devices  36.2 us (19%)
  Pallas kernels  34.6 us (18%)
  waiting for transfers between devices  26.4 us (14%)
  local copies, waits for them, and re-layouts  2.25 us (1%)
    all_to_all x4, blocking collectives, exchange(): return lax.all_to_all(blocks, axes, 0, 0, tiled=True)  85.6 us
    pallas_call x11, Pallas kernels, local_call(): pl.pallas_call(kernel, out_shape=[s if isinstance(s, jax.ShapeDtypeStruct...  34.6 us
    all_to_all x4, waiting for transfers between devices, exchange(): return lax.all_to_all(blocks, axes, 0, 0, tiled=True)  23.9 us
    all_to_all x4, starting transfers between devices, exchange(): return lax.all_to_all(blocks, axes, 0, 0, tiled=True)  20.6 us
    ppermute x3, starting transfers between devices, gather_all(): return (own, lax.ppermute(own, 'core', [(0, 1), (1, 0)]))  15.6 us
  transfers between devices with their start and end apart: 7, of which 6 were waited for; matrix products, arithmetic and copies ran while one was open for 1% of the time, Pallas kernels for 15%

commit v1 on v0

--- a/solution.py
+++ b/solution.py
@@ -187,11 +187,6 @@
     next_ref[...] = next_ref[...] * by_row
 
 
-def given_copies_kernel(b_ref, c_ref, out_ref):
-    row = jnp.concatenate([b_ref[...], c_ref[...]], axis=1)
-    out_ref[...] = jnp.broadcast_to(row[None], out_ref.shape)
-
-
 def spread_kernel(parts_ref, *refs):
     out_ref = refs[-1]
     total = jnp.sum(parts_ref[...], axis=0)
@@ -235,7 +230,7 @@
     return lax.all_to_all(blocks, axes, 0, 0, tiled=True)
 
 
-COL = ("col_hi", "col_lo")
+COL = ("col",)
 PLANE = ("aa", "y") + COL
 
 
@@ -247,18 +242,17 @@
 def body(tensor, b_row, c_row):
     blk_i, blk_j, blk_k = tensor.shape
     rank = b_row.shape[1]
-    n_aa, n_y, n_core, n_hi = (lax.axis_size(axis) for axis in ("aa", "y", "core", "col_hi"))
-    n_col = axes_size(COL)
+    n_aa, n_y, n_core, n_col = (lax.axis_size(axis) for axis in ("aa", "y", "core", "col"))
     aa, y, core, col = (lax.axis_index(axis) for axis in ("aa", "y", "core", COL))
     place = jnp.stack([aa, y, core, col]).astype(jnp.int32)
     square, heavy = (rank, rank), 12 * 10**9
     planes = axes_size(PLANE)
     a_parts = (n_aa * n_y, blk_i // (n_y * n_core), rank)
-    b_parts = (n_y * n_hi, blk_j // n_hi, rank)
+    b_parts = (n_y * n_col, blk_j // n_col, rank)
     low = lambda rows: jax.ShapeDtypeStruct((rows, rank), jnp.bfloat16)
 
-    copies = local_call(given_copies_kernel, [(planes, 1, 2 * rank)], b_row, c_row)[0]
-    own, other = gather_all(copies, PLANE)
+    given = jnp.concatenate([b_row, c_row], axis=1)[None]
+    own, other = gather_all(jnp.broadcast_to(given, (planes, 1, 2 * rank)), PLANE)
     c_block, partial = local_call(
         first_kernel, [low(blk_k), (n_y * n_core * n_col,) + a_parts[1:]], tensor, own, other, flops=4 * 10**9, place=place
     )
@@ -279,7 +273,7 @@
         own, other, solve, gram_c, raw_a, row, partial,
         flops=heavy, waits=1,
     )
-    own, other = gather_all(local_call(spread_kernel, [b_parts], parts, solve, waits=1)[0], ("y", "col_hi"))
+    own, other = gather_all(local_call(spread_kernel, [b_parts], parts, solve, waits=1)[0], ("y",) + COL)
     raw_b = dot(lax.dynamic_slice_in_dim(own, y * blk_j, blk_j, 0), solve)
 
     inner = jnp.einsum("ijk,ir->jkr", tensor, a_low, preferred_element_type=F32)
@@ -303,9 +297,7 @@
 
 def solution(mesh):
     n_aa, n_ba, n_col = mesh.devices.shape
-    fine = Mesh(
-        mesh.devices.reshape(n_aa, n_ba // 2, 2, n_col // 2, 2), ("aa", "y", "core", "col_hi", "col_lo")
-    )
+    fine = Mesh(mesh.devices.reshape(n_aa, n_ba // 2, 2, n_col), ("aa", "y", "core", "col"))
     a_spec = P(("aa", "y", "core") + COL, None)
     b_spec = P(("y", "core", "aa") + COL, None)
     c_spec = P(COL + ("aa", "y", "core"), None)

time: 188 us -> 185 us (0.984)
  waiting for transfers between devices: 26.4 us -> 20.9 us
  starting transfers between devices: 36.2 us -> 38.1 us
    all_to_all x4, waiting for transfers between devices: 23.9 us -> 18.3 us  [exchange(): return lax.all_to_all(blocks, axes, 0, 0, tiled=True)]
    all_to_all x4, starting transfers between devices: 20.6 us -> 22.5 us  [exchange(): return lax.all_to_all(blocks, axes, 0, 0, tiled=True)]
    pallas_call x11 -> x10, Pallas kernels: 34.6 us -> 34.4 us  [local_call(): pl.pallas_call(kernel, out_shape=[s if isinstance(s, jax.ShapeDtypeStruct...]
  transfers between devices with their start and end apart: 7 -> 7, of which waited for: 6 -> 6; matrix products, arithmetic and copies ran while one was open for 1% -> 1% of each run, Pallas kernels for 15% -> 16%
where the time goes in v1:
time: 185 us; the launch traced here: 184 us
  blocking collectives  86.5 us (47%)
  starting transfers between devices  38.1 us (21%)
  Pallas kernels  34.4 us (19%)
  waiting for transfers between devices  20.9 us (11%)
    all_to_all x4, blocking collectives, exchange(): return lax.all_to_all(blocks, axes, 0, 0, tiled=True)  86.5 us
    pallas_call x10, Pallas kernels, local_call(): pl.pallas_call(kernel, out_shape=[s if isinstance(s, jax.ShapeDtypeStruct...  34.4 us
    all_to_all x4, starting transfers between devices, exchange(): return lax.all_to_all(blocks, axes, 0, 0, tiled=True)  22.5 us
    all_to_all x4, waiting for transfers between devices, exchange(): return lax.all_to_all(blocks, axes, 0, 0, tiled=True)  18.3 us
    ppermute x3, starting transfers between devices, gather_all(): return (own, lax.ppermute(own, 'core', [(0, 1), (1, 0)]))  15.6 us
  transfers between devices with their start and end apart: 7, of which 6 were waited for; matrix products, arithmetic and copies ran while one was open for 1% of the time, Pallas kernels for 16%

profile of v1, /device:TPU:1, one launch (start us, length us, event | category | flops | bytes accessed | tf_op | source)
XLA Modules:
  0.0 184.4 jit_solution(7598404670772919168)
XLA Ops:
  0.6 0.7 pad_maximum_fusion
  1.3 0.3 broadcast_in_dim.10
  1.6 40.5 %all_to_all.40 = f32[256,1,512]{2,1,0:T(1,128)S(1)} all-to-all(f32[256,1,512]{2,1,0:T(1,128)S(1)} %broadcast_in_dim.10), channel_id=1, replica_groups=mesh['aa'=8,'y'=8,'core'=2,'col'=4] {'aa','y','col'}, dimensions={0} | all-to-all | bytes 1048576 | tf_op jit(solution)/shard_map/all_to_all | solution.py:230
  42.1 0.0 copy-start
  42.2 5.2 %collective-permute-start = (f32[256,512]{1,0:T(8,128)S(1)}, f32[256,512]{1,0:T(8,128)S(1)}, u32[]{:S(2)}, u32[]{:S(2)}) collective-permute-start(f32[256,512]{1,0:T(8,128)S(1)} %bitcast.18), channel_id=1, source_target_pairs={{0,4},{4,0},{1,5},{5,1},{2,6},{6,2},{3,7},{7,3},{8,12},{12,8},{9,1... | collective-permute-start | bytes 1572872 | tf_op jit(solution)/shard_map/ppermute | solution.py:239
  47.4 0.1 pad_add_fusion.place_ref
  47.5 1.4 collective-permute-done.other_ref
  48.9 0.0 copy-done
  49.0 2.0 %shard_map.58 = (bf16[128,256]{1,0:T(8,128)(2,1)S(1)}, f32[64,4,256]{2,1,0:T(4,128)}) custom-call(s32[4]{0:T(128)S(1)} %pad_add_fusion.place_ref, bf16[64,32,128]{2,1,0:T(8,128)(2,1)S(1)} %copy-done, f32[256,512]{1,0:T(8,128)S(1)} %bitcast.19, f32[256,512]{1,0:T(8,128)S(1)} %collective-permute-done.other_ref), custom_call_target="tpu_custom_call" | custom-call | flops 4000000000 | bytes 1048576 | tf_op jit(solution)/shard_map/pallas_call | solution.py:212
  50.9 5.5 %all-to-all-start.1 = ((f32[64,4,256]{2,1,0:T(4,128)}), f32[64,4,256]{2,1,0:T(4,128)S(1)}, u32[]{:S(2)}, u32[]{:S(2)}) async-start(f32[64,4,256]{2,1,0:T(4,128)} %get-tuple-element.18._), calls=%async_computation.1 | async-start | bytes 524288 | tf_op jit(solution)/shard_map/all_to_all | solution.py:230
  56.5 9.1 %shard_map.59 = (f32[256,256]{1,0:T(8,128)S(1)}, f32[256,256]{1,0:T(8,128)S(1)}) custom-call(f32[256,512]{1,0:T(8,128)S(1)} %bitcast.20, f32[256,512]{1,0:T(8,128)S(1)} %collective-permute-done.other_ref, f32[64,4,256]{2,1,0:T(4,128)} %get-tuple-element.18._), custom_call_target="tpu_custom_call" | custom-call | flops 12000000000 | bytes 1048576 | tf_op jit(solution)/shard_map/pallas_call | solution.py:212
  65.6 3.1 %all-to-all-done.1.parts_ref = f32[64,4,256]{2,1,0:T(4,128)S(1)} async-done(((f32[64,4,256]{2,1,0:T(4,128)}), f32[64,4,256]{2,1,0:T(4,128)S(1)}, u32[]{:S(2)}, u32[]{:S(2)}) %all-to-all-start.1) | async-done | bytes 262176 | tf_op jit(solution)/shard_map/all_to_all | solution.py:230
  68.7 0.1 shard_map.60
  68.8 18.1 %all_to_all.41 = f32[64,4,256]{2,1,0:T(4,128)S(1)} all-to-all(f32[64,4,256]{2,1,0:T(4,128)S(1)} %shard_map.60), channel_id=1, replica_groups=mesh['aa'=8,'y'=8,'core'=2,'col'=4] {'aa','y'}, dimensions={0} | all-to-all | bytes 524288 | tf_op jit(solution)/shard_map/all_to_all | solution.py:230
  86.9 0.1 reshape.23.own_ref
  87.0 4.9 %collective-permute-start.1 = (f32[256,256]{1,0:T(8,128)S(1)}, f32[256,256]{1,0:T(8,128)S(1)}, u32[]{:S(2)}, u32[]{:S(2)}) collective-permute-start(f32[256,256]{1,0:T(8,128)S(1)} %reshape.23.own_ref), channel_id=1, source_target_pairs={{0,4},{4,0},{1,5},{5,1},{2,6},{6,2},{3,7},{7,3},{8,12},{12,8},{9,1... | collective-permute-start | bytes 786440 | tf_op jit(solution)/shard_map/ppermute | solution.py:239
  91.9 1.1 collective-permute-done.1.other_ref
  93.1 1.9 %shard_map.61 = (f32[64,256]{1,0:T(8,128)S(1)}, f32[1,256]{1,0:T(1,128)S(1)}, f32[32,8,256]{2,1,0:T(8,128)}) custom-call(s32[4]{0:T(128)S(1)} %pad_add_fusion.place_ref, bf16[64,32,128]{2,1,0:T(8,128)(2,1)S(1)} %copy-done, bf16[128,256]{1,0:T(8,128)(2,1)S(1)} %get-tuple-element.21.c_block_ref, f32[256,256]{1,0:T(8,128)S(1)} %reshape.23.own_ref, ...), custom_call_target="tpu_custom_call" | custom-call | flops 4000000000 | bytes 1048576 | tf_op jit(solution)/shard_map/pallas_call | solution.py:212
  95.0 5.6 %all-to-all-start.3 = ((f32[32,8,256]{2,1,0:T(8,128)}), f32[32,8,256]{2,1,0:T(8,128)S(1)}, u32[]{:S(2)}, u32[]{:S(2)}) async-start(f32[32,8,256]{2,1,0:T(8,128)} %get-tuple-element.24._), calls=%async_computation.3 | async-start | bytes 524288 | tf_op jit(solution)/shard_map/all_to_all | solution.py:230
  100.6 9.7 %shard_map.62 = (f32[256,256]{1,0:T(8,128)S(1)}, f32[256,256]{1,0:T(8,128)S(1)}, bf16[64,256]{1,0:T(8,128)(2,1)S(1)}, f32[1,256]{1,0:T(1,128)}) custom-call(f32[256,256]{1,0:T(8,128)S(1)} %reshape.23.own_ref, f32[256,256]{1,0:T(8,128)S(1)} %collective-permute-done.1.other_ref, f32[256,256]{1,0:T(8,128)S(1)} %get-tuple-element.19.refs_0_.solve_ref, ...), custom_call_target="tpu_custom_call" | custom-call | flops 12000000000 | bytes 1048576 | tf_op jit(solution)/shard_map/pallas_call | solution.py:212
  110.3 1.6 all-to-all-done.3.parts_ref
  111.9 0.7 shard_map.63
  112.7 3.9 %all-to-all-start.4 = ((f32[32,8,256]{2,1,0:T(8,128)}), f32[32,8,256]{2,1,0:T(8,128)S(1)}, u32[]{:S(2)}, u32[]{:S(2)}) async-start(f32[32,8,256]{2,1,0:T(8,128)} %shard_map.63), calls=%async_computation.4 | async-start | bytes 524288 | tf_op jit(solution)/shard_map/all_to_all | solution.py:230
  116.6 10.6 %all-to-all-done.4 = f32[32,8,256]{2,1,0:T(8,128)S(1)} async-done(((f32[32,8,256]{2,1,0:T(8,128)}), f32[32,8,256]{2,1,0:T(8,128)S(1)}, u32[]{:S(2)}, u32[]{:S(2)}) %all-to-all-start.4) | async-done | bytes 262176 | tf_op jit(solution)/shard_map/all_to_all | solution.py:230
  127.2 5.5 %collective-permute-start.2 = (f32[256,256]{1,0:T(8,128)S(1)}, f32[256,256]{1,0:T(8,128)S(1)}, u32[]{:S(2)}, u32[]{:S(2)}) collective-permute-start(f32[256,256]{1,0:T(8,128)S(1)} %bitcast.21), channel_id=1, source_target_pairs={{0,4},{4,0},{1,5},{5,1},{2,6},{6,2},{3,7},{7,3},{8,12},{12,8},{9,1... | collective-permute-start | bytes 786440 | tf_op jit(solution)/shard_map/ppermute | solution.py:239
  132.6 0.2 fusion.6.block_ref
  132.9 1.5 fusion
  134.4 0.8 copy.9._
  135.2 7.5 %all-to-all-start.5 = ((f32[128,1,256]{2,1,0:T(1,128)}), f32[128,1,256]{2,1,0:T(1,128)S(1)}, u32[]{:S(2)}, u32[]{:S(2)}) async-start(f32[128,1,256]{2,1,0:T(1,128)} %copy.9._), calls=%async_computation.5 | async-start | bytes 262144 | tf_op jit(solution)/shard_map/all_to_all | solution.py:230
  142.7 0.0 collective-permute-done.2.other_ref
  142.7 9.7 %shard_map.64 = (f32[256,256]{1,0:T(8,128)S(1)}, f32[256,256]{1,0:T(8,128)}, bf16[32,256]{1,0:T(8,128)(2,1)}, f32[1,256]{1,0:T(1,128)}) custom-call(f32[256,256]{1,0:T(8,128)S(1)} %bitcast.23, f32[256,256]{1,0:T(8,128)S(1)} %collective-permute-done.2.other_ref, f32[256,256]{1,0:T(8,128)S(1)} %get-tuple-element.26.refs_0_.solve_ref, ...), custom_call_target="tpu_custom_call" | custom-call | flops 12000000000 | bytes 1048576 | tf_op jit(solution)/shard_map/pallas_call | solution.py:212
  152.5 3.0 %all-to-all-done.5.parts_ref = f32[128,1,256]{2,1,0:T(1,128)S(1)} async-done(((f32[128,1,256]{2,1,0:T(1,128)}), f32[128,1,256]{2,1,0:T(1,128)S(1)}, u32[]{:S(2)}, u32[]{:S(2)}) %all-to-all-start.5) | async-done | bytes 131104 | tf_op jit(solution)/shard_map/all_to_all | solution.py:230
  155.5 0.4 shard_map.65
  155.8 11.7 %all_to_all.42.parts_ref = f32[16,1,256]{2,1,0:T(1,128)S(1)} all-to-all(f32[16,1,256]{2,1,0:T(1,128)S(1)} %get-tuple-element.31), channel_id=1, replica_groups=mesh['aa'=8,'y'=8,'core'=2,'col'=4] {'aa','core'}, dimensions={0} | all-to-all | bytes 32768 | tf_op jit(solution)/shard_map/all_to_all | solution.py:230
  167.6 16.2 %all_to_all.43.parts_ref = f32[32,1,256]{2,1,0:T(1,128)S(1)} all-to-all(f32[32,1,256]{2,1,0:T(1,128)S(1)} %shard_map.66), channel_id=1, replica_groups=mesh['aa'=8,'y'=8,'core'=2,'col'=4] {'y','col'}, dimensions={0} | all-to-all | bytes 65536 | tf_op jit(solution)/shard_map/all_to_all | solution.py:230
  183.7 0.6 shard_map.67
  (3 shorter events, 0.1 us)
Async XLA Ops:
  42.1 6.8 %copy-start = (bf16[64,32,128]{2,1,0:T(8,128)(2,1)S(1)}, bf16[64,32,128]{2,1,0:T(8,128)(2,1)}, u32[]{:S(2)}) copy-start(bf16[64,32,128]{2,1,0:T(8,128)(2,1)} %tensor_ref.3) | copy-start | bytes 1572868
  42.2 6.8 %collective-permute-start = (f32[256,512]{1,0:T(8,128)S(1)}, f32[256,512]{1,0:T(8,128)S(1)}, u32[]{:S(2)}, u32[]{:S(2)}) collective-permute-start(f32[256,512]{1,0:T(8,128)S(1)} %bitcast.18), channel_id=1, source_target_pairs={{0,4},{4,0},{1,5},{5,1},{2,6},{6,2},{3,7},{7,3},{8,12},{12,8},{9,1... | collective-permute-start | bytes 1572872 | tf_op jit(solution)/shard_map/ppermute | solution.py:239
  50.9 17.8 %all-to-all-start.1 = ((f32[64,4,256]{2,1,0:T(4,128)}), f32[64,4,256]{2,1,0:T(4,128)S(1)}, u32[]{:S(2)}, u32[]{:S(2)}) async-start(f32[64,4,256]{2,1,0:T(4,128)} %get-tuple-element.18._), calls=%async_computation.1 | async-start | bytes 524288 | tf_op jit(solution)/shard_map/all_to_all | solution.py:230
  87.0 6.0 %collective-permute-start.1 = (f32[256,256]{1,0:T(8,128)S(1)}, f32[256,256]{1,0:T(8,128)S(1)}, u32[]{:S(2)}, u32[]{:S(2)}) collective-permute-start(f32[256,256]{1,0:T(8,128)S(1)} %reshape.23.own_ref), channel_id=1, source_target_pairs={{0,4},{4,0},{1,5},{5,1},{2,6},{6,2},{3,7},{7,3},{8,12},{12,8},{9,1... | collective-permute-start | bytes 786440 | tf_op jit(solution)/shard_map/ppermute | solution.py:239
  95.0 16.9 %all-to-all-start.3 = ((f32[32,8,256]{2,1,0:T(8,128)}), f32[32,8,256]{2,1,0:T(8,128)S(1)}, u32[]{:S(2)}, u32[]{:S(2)}) async-start(f32[32,8,256]{2,1,0:T(8,128)} %get-tuple-element.24._), calls=%async_computation.3 | async-start | bytes 524288 | tf_op jit(solution)/shard_map/all_to_all | solution.py:230
  112.7 14.5 %all-to-all-start.4 = ((f32[32,8,256]{2,1,0:T(8,128)}), f32[32,8,256]{2,1,0:T(8,128)S(1)}, u32[]{:S(2)}, u32[]{:S(2)}) async-start(f32[32,8,256]{2,1,0:T(8,128)} %shard_map.63), calls=%async_computation.4 | async-start | bytes 524288 | tf_op jit(solution)/shard_map/all_to_all | solution.py:230
  127.2 15.6 %collective-permute-start.2 = (f32[256,256]{1,0:T(8,128)S(1)}, f32[256,256]{1,0:T(8,128)S(1)}, u32[]{:S(2)}, u32[]{:S(2)}) collective-permute-start(f32[256,256]{1,0:T(8,128)S(1)} %bitcast.21), channel_id=1, source_target_pairs={{0,4},{4,0},{1,5},{5,1},{2,6},{6,2},{3,7},{7,3},{8,12},{12,8},{9,1... | collective-permute-start | bytes 786440 | tf_op jit(solution)/shard_map/ppermute | solution.py:239
  135.2 20.3 %all-to-all-start.5 = ((f32[128,1,256]{2,1,0:T(1,128)}), f32[128,1,256]{2,1,0:T(1,128)S(1)}, u32[]{:S(2)}, u32[]{:S(2)}) async-start(f32[128,1,256]{2,1,0:T(1,128)} %copy.9._), calls=%async_computation.5 | async-start | bytes 262144 | tf_op jit(solution)/shard_map/all_to_all | solution.py:230

commit v2 on v1

--- a/solution.py
+++ b/solution.py
@@ -127,10 +127,13 @@
     for lo in range(0, blk_i, ROWS):
         flat = tensor_ref[lo : lo + ROWS].reshape(ROWS * blk_j, blk_k)
         inner = jnp.dot(flat, c_block, preferred_element_type=F32)
-        for i in range(lo, lo + ROWS):
-            row = jnp.sum(inner[(i - lo) * blk_j : (i - lo + 1) * blk_j] * b_block, axis=0, keepdims=True)
+        rows = [
+            jnp.sum(inner[i * blk_j : (i + 1) * blk_j] * b_block, axis=0, keepdims=True) for i in range(ROWS)
+        ]
+        for i in range(0, ROWS, n_col):
+            group = jnp.concatenate(rows[i : i + n_col], axis=0)
             for copy in range(n_col):
-                out_ref[i // n_col * n_col + copy, i % n_col : i % n_col + 1, :] = row
+                out_ref[lo + i + copy] = group
 
 
 def second_kernel(place_ref, tensor_ref, c_block_ref, own_ref, other_ref, solve_ref, raw_ref, row_ref, out_ref):
@@ -287,7 +290,7 @@
         flops=heavy, waits=1,
     )
 
-    near, far = ("aa", "core"), ("y",) + COL
+    near, far = ("y",) + COL, ("aa", "core")
     raw_c, squares = local_call(apply_kernel, [(1, rank), (axes_size(near), 1, rank)], parts, solve)
     squares = local_call(spread_kernel, [(axes_size(far), 1, rank)], exchange(squares, near))[0]
     scale = functools.partial(scale_kernel, blk_k * n_col)

time: 185 us -> 186 us (level)
  transfers between devices with their start and end apart: 7 -> 7, of which waited for: 6 -> 6; matrix products, arithmetic and copies ran while one was open for 1% -> 1% of each run, Pallas kernels for 16% -> 15%
where the time goes in v2:
time: 186 us
  blocking collectives  87.9 us (47%)
  starting transfers between devices  38.1 us (20%)
  Pallas kernels  34.4 us (18%)
  waiting for transfers between devices  20.9 us (11%)
    all_to_all x4, blocking collectives, exchange(): return lax.all_to_all(blocks, axes, 0, 0, tiled=True)  87.9 us
    pallas_call x10, Pallas kernels, local_call(): pl.pallas_call(kernel, out_shape=[s if isinstance(s, jax.ShapeDtypeStruct...  34.4 us
    all_to_all x4, starting transfers between devices, exchange(): return lax.all_to_all(blocks, axes, 0, 0, tiled=True)  22.5 us
    all_to_all x4, waiting for transfers between devices, exchange(): return lax.all_to_all(blocks, axes, 0, 0, tiled=True)  18.3 us
    ppermute x3, starting transfers between devices, gather_all(): return (own, lax.ppermute(own, 'core', [(0, 1), (1, 0)]))  15.6 us
  transfers between devices with their start and end apart: 7, of which 6 were waited for; matrix products, arithmetic and copies ran while one was open for 1% of the time, Pallas kernels for 15%

profile of v2, /device:TPU:1, one launch (start us, length us, event | category | flops | bytes accessed | tf_op | source)
XLA Modules:
  0.0 185.7 jit_solution(6581361421770641030)
XLA Ops:
  0.6 0.7 pad_maximum_fusion
  1.3 0.3 broadcast_in_dim.10
  1.6 40.5 %all_to_all.40 = f32[256,1,512]{2,1,0:T(1,128)S(1)} all-to-all(f32[256,1,512]{2,1,0:T(1,128)S(1)} %broadcast_in_dim.10), channel_id=1, replica_groups=mesh['aa'=8,'y'=8,'core'=2,'col'=4] {'aa','y','col'}, dimensions={0} | all-to-all | bytes 1048576 | tf_op jit(solution)/shard_map/all_to_all | solution.py:233
  42.1 0.0 copy-start
  42.2 5.2 %collective-permute-start = (f32[256,512]{1,0:T(8,128)S(1)}, f32[256,512]{1,0:T(8,128)S(1)}, u32[]{:S(2)}, u32[]{:S(2)}) collective-permute-start(f32[256,512]{1,0:T(8,128)S(1)} %bitcast.18), channel_id=1, source_target_pairs={{0,4},{4,0},{1,5},{5,1},{2,6},{6,2},{3,7},{7,3},{8,12},{12,8},{9,1... | collective-permute-start | bytes 1572872 | tf_op jit(solution)/shard_map/ppermute | solution.py:242
  47.4 0.1 pad_add_fusion.place_ref
  47.5 1.4 collective-permute-done.other_ref
  48.9 0.0 copy-done
  49.0 2.0 %shard_map.58 = (bf16[128,256]{1,0:T(8,128)(2,1)S(1)}, f32[64,4,256]{2,1,0:T(4,128)}) custom-call(s32[4]{0:T(128)S(1)} %pad_add_fusion.place_ref, bf16[64,32,128]{2,1,0:T(8,128)(2,1)S(1)} %copy-done, f32[256,512]{1,0:T(8,128)S(1)} %bitcast.19, f32[256,512]{1,0:T(8,128)S(1)} %collective-permute-done.other_ref), custom_call_target="tpu_custom_call" | custom-call | flops 4000000000 | bytes 1048576 | tf_op jit(solution)/shard_map/pallas_call | solution.py:215
  50.9 5.5 %all-to-all-start.1 = ((f32[64,4,256]{2,1,0:T(4,128)}), f32[64,4,256]{2,1,0:T(4,128)S(1)}, u32[]{:S(2)}, u32[]{:S(2)}) async-start(f32[64,4,256]{2,1,0:T(4,128)} %get-tuple-element.18._), calls=%async_computation.1 | async-start | bytes 524288 | tf_op jit(solution)/shard_map/all_to_all | solution.py:233
  56.5 9.1 %shard_map.59 = (f32[256,256]{1,0:T(8,128)S(1)}, f32[256,256]{1,0:T(8,128)S(1)}) custom-call(f32[256,512]{1,0:T(8,128)S(1)} %bitcast.20, f32[256,512]{1,0:T(8,128)S(1)} %collective-permute-done.other_ref, f32[64,4,256]{2,1,0:T(4,128)} %get-tuple-element.18._), custom_call_target="tpu_custom_call" | custom-call | flops 12000000000 | bytes 1048576 | tf_op jit(solution)/shard_map/pallas_call | solution.py:215
  65.6 3.1 %all-to-all-done.1.parts_ref = f32[64,4,256]{2,1,0:T(4,128)S(1)} async-done(((f32[64,4,256]{2,1,0:T(4,128)}), f32[64,4,256]{2,1,0:T(4,128)S(1)}, u32[]{:S(2)}, u32[]{:S(2)}) %all-to-all-start.1) | async-done | bytes 262176 | tf_op jit(solution)/shard_map/all_to_all | solution.py:233
  68.7 0.1 shard_map.60
  68.8 18.1 %all_to_all.41 = f32[64,4,256]{2,1,0:T(4,128)S(1)} all-to-all(f32[64,4,256]{2,1,0:T(4,128)S(1)} %shard_map.60), channel_id=1, replica_groups=mesh['aa'=8,'y'=8,'core'=2,'col'=4] {'aa','y'}, dimensions={0} | all-to-all | bytes 524288 | tf_op jit(solution)/shard_map/all_to_all | solution.py:233
  86.9 0.1 reshape.23.own_ref
  87.0 4.9 %collective-permute-start.1 = (f32[256,256]{1,0:T(8,128)S(1)}, f32[256,256]{1,0:T(8,128)S(1)}, u32[]{:S(2)}, u32[]{:S(2)}) collective-permute-start(f32[256,256]{1,0:T(8,128)S(1)} %reshape.23.own_ref), channel_id=1, source_target_pairs={{0,4},{4,0},{1,5},{5,1},{2,6},{6,2},{3,7},{7,3},{8,12},{12,8},{9,1... | collective-permute-start | bytes 786440 | tf_op jit(solution)/shard_map/ppermute | solution.py:242
  91.9 1.1 collective-permute-done.1.other_ref
  93.1 1.9 %shard_map.61 = (f32[64,256]{1,0:T(8,128)S(1)}, f32[1,256]{1,0:T(1,128)S(1)}, f32[32,8,256]{2,1,0:T(8,128)}) custom-call(s32[4]{0:T(128)S(1)} %pad_add_fusion.place_ref, bf16[64,32,128]{2,1,0:T(8,128)(2,1)S(1)} %copy-done, bf16[128,256]{1,0:T(8,128)(2,1)S(1)} %get-tuple-element.21.c_block_ref, f32[256,256]{1,0:T(8,128)S(1)} %reshape.23.own_ref, ...), custom_call_target="tpu_custom_call" | custom-call | flops 4000000000 | bytes 1048576 | tf_op jit(solution)/shard_map/pallas_call | solution.py:215
  95.0 5.6 %all-to-all-start.3 = ((f32[32,8,256]{2,1,0:T(8,128)}), f32[32,8,256]{2,1,0:T(8,128)S(1)}, u32[]{:S(2)}, u32[]{:S(2)}) async-start(f32[32,8,256]{2,1,0:T(8,128)} %get-tuple-element.24._), calls=%async_computation.3 | async-start | bytes 524288 | tf_op jit(solution)/shard_map/all_to_all | solution.py:233
  100.6 9.7 %shard_map.62 = (f32[256,256]{1,0:T(8,128)S(1)}, f32[256,256]{1,0:T(8,128)S(1)}, bf16[64,256]{1,0:T(8,128)(2,1)S(1)}, f32[1,256]{1,0:T(1,128)}) custom-call(f32[256,256]{1,0:T(8,128)S(1)} %reshape.23.own_ref, f32[256,256]{1,0:T(8,128)S(1)} %collective-permute-done.1.other_ref, f32[256,256]{1,0:T(8,128)S(1)} %get-tuple-element.19.refs_0_.solve_ref, ...), custom_call_target="tpu_custom_call" | custom-call | flops 12000000000 | bytes 1048576 | tf_op jit(solution)/shard_map/pallas_call | solution.py:215
  110.3 1.6 all-to-all-done.3.parts_ref
  111.9 0.7 shard_map.63
  112.7 3.9 %all-to-all-start.4 = ((f32[32,8,256]{2,1,0:T(8,128)}), f32[32,8,256]{2,1,0:T(8,128)S(1)}, u32[]{:S(2)}, u32[]{:S(2)}) async-start(f32[32,8,256]{2,1,0:T(8,128)} %shard_map.63), calls=%async_computation.4 | async-start | bytes 524288 | tf_op jit(solution)/shard_map/all_to_all | solution.py:233
  116.6 10.6 %all-to-all-done.4 = f32[32,8,256]{2,1,0:T(8,128)S(1)} async-done(((f32[32,8,256]{2,1,0:T(8,128)}), f32[32,8,256]{2,1,0:T(8,128)S(1)}, u32[]{:S(2)}, u32[]{:S(2)}) %all-to-all-start.4) | async-done | bytes 262176 | tf_op jit(solution)/shard_map/all_to_all | solution.py:233
  127.2 5.5 %collective-permute-start.2 = (f32[256,256]{1,0:T(8,128)S(1)}, f32[256,256]{1,0:T(8,128)S(1)}, u32[]{:S(2)}, u32[]{:S(2)}) collective-permute-start(f32[256,256]{1,0:T(8,128)S(1)} %bitcast.21), channel_id=1, source_target_pairs={{0,4},{4,0},{1,5},{5,1},{2,6},{6,2},{3,7},{7,3},{8,12},{12,8},{9,1... | collective-permute-start | bytes 786440 | tf_op jit(solution)/shard_map/ppermute | solution.py:242
  132.6 0.2 fusion.6.block_ref
  132.9 1.5 fusion
  134.4 0.8 copy.9._
  135.2 7.5 %all-to-all-start.5 = ((f32[128,1,256]{2,1,0:T(1,128)}), f32[128,1,256]{2,1,0:T(1,128)S(1)}, u32[]{:S(2)}, u32[]{:S(2)}) async-start(f32[128,1,256]{2,1,0:T(1,128)} %copy.9._), calls=%async_computation.5 | async-start | bytes 262144 | tf_op jit(solution)/shard_map/all_to_all | solution.py:233
  142.7 0.0 collective-permute-done.2.other_ref
  142.7 9.7 %shard_map.64 = (f32[256,256]{1,0:T(8,128)S(1)}, f32[256,256]{1,0:T(8,128)}, bf16[32,256]{1,0:T(8,128)(2,1)}, f32[1,256]{1,0:T(1,128)}) custom-call(f32[256,256]{1,0:T(8,128)S(1)} %bitcast.23, f32[256,256]{1,0:T(8,128)S(1)} %collective-permute-done.2.other_ref, f32[256,256]{1,0:T(8,128)S(1)} %get-tuple-element.26.refs_0_.solve_ref, ...), custom_call_target="tpu_custom_call" | custom-call | flops 12000000000 | bytes 1048576 | tf_op jit(solution)/shard_map/pallas_call | solution.py:215
  152.5 3.0 %all-to-all-done.5.parts_ref = f32[128,1,256]{2,1,0:T(1,128)S(1)} async-done(((f32[128,1,256]{2,1,0:T(1,128)}), f32[128,1,256]{2,1,0:T(1,128)S(1)}, u32[]{:S(2)}, u32[]{:S(2)}) %all-to-all-start.5) | async-done | bytes 131104 | tf_op jit(solution)/shard_map/all_to_all | solution.py:233
  155.5 0.4 shard_map.65
  155.8 13.4 %all_to_all.42.parts_ref = f32[32,1,256]{2,1,0:T(1,128)S(1)} all-to-all(f32[32,1,256]{2,1,0:T(1,128)S(1)} %get-tuple-element.31), channel_id=1, replica_groups=mesh['aa'=8,'y'=8,'core'=2,'col'=4] {'y','col'}, dimensions={0} | all-to-all | bytes 65536 | tf_op jit(solution)/shard_map/all_to_all | solution.py:233
  169.3 15.9 %all_to_all.43.parts_ref = f32[16,1,256]{2,1,0:T(1,128)S(1)} all-to-all(f32[16,1,256]{2,1,0:T(1,128)S(1)} %shard_map.66), channel_id=1, replica_groups=mesh['aa'=8,'y'=8,'core'=2,'col'=4] {'aa','core'}, dimensions={0} | all-to-all | bytes 32768 | tf_op jit(solution)/shard_map/all_to_all | solution.py:233
  185.1 0.6 shard_map.67
  (3 shorter events, 0.1 us)
Async XLA Ops:
  42.1 6.8 %copy-start = (bf16[64,32,128]{2,1,0:T(8,128)(2,1)S(1)}, bf16[64,32,128]{2,1,0:T(8,128)(2,1)}, u32[]{:S(2)}) copy-start(bf16[64,32,128]{2,1,0:T(8,128)(2,1)} %tensor_ref.3) | copy-start | bytes 1572868
  42.2 6.8 %collective-permute-start = (f32[256,512]{1,0:T(8,128)S(1)}, f32[256,512]{1,0:T(8,128)S(1)}, u32[]{:S(2)}, u32[]{:S(2)}) collective-permute-start(f32[256,512]{1,0:T(8,128)S(1)} %bitcast.18), channel_id=1, source_target_pairs={{0,4},{4,0},{1,5},{5,1},{2,6},{6,2},{3,7},{7,3},{8,12},{12,8},{9,1... | collective-permute-start | bytes 1572872 | tf_op jit(solution)/shard_map/ppermute | solution.py:242
  50.9 17.8 %all-to-all-start.1 = ((f32[64,4,256]{2,1,0:T(4,128)}), f32[64,4,256]{2,1,0:T(4,128)S(1)}, u32[]{:S(2)}, u32[]{:S(2)}) async-start(f32[64,4,256]{2,1,0:T(4,128)} %get-tuple-element.18._), calls=%async_computation.1 | async-start | bytes 524288 | tf_op jit(solution)/shard_map/all_to_all | solution.py:233
  87.0 6.0 %collective-permute-start.1 = (f32[256,256]{1,0:T(8,128)S(1)}, f32[256,256]{1,0:T(8,128)S(1)}, u32[]{:S(2)}, u32[]{:S(2)}) collective-permute-start(f32[256,256]{1,0:T(8,128)S(1)} %reshape.23.own_ref), channel_id=1, source_target_pairs={{0,4},{4,0},{1,5},{5,1},{2,6},{6,2},{3,7},{7,3},{8,12},{12,8},{9,1... | collective-permute-start | bytes 786440 | tf_op jit(solution)/shard_map/ppermute | solution.py:242
  95.0 16.9 %all-to-all-start.3 = ((f32[32,8,256]{2,1,0:T(8,128)}), f32[32,8,256]{2,1,0:T(8,128)S(1)}, u32[]{:S(2)}, u32[]{:S(2)}) async-start(f32[32,8,256]{2,1,0:T(8,128)} %get-tuple-element.24._), calls=%async_computation.3 | async-start | bytes 524288 | tf_op jit(solution)/shard_map/all_to_all | solution.py:233
  112.7 14.5 %all-to-all-start.4 = ((f32[32,8,256]{2,1,0:T(8,128)}), f32[32,8,256]{2,1,0:T(8,128)S(1)}, u32[]{:S(2)}, u32[]{:S(2)}) async-start(f32[32,8,256]{2,1,0:T(8,128)} %shard_map.63), calls=%async_computation.4 | async-start | bytes 524288 | tf_op jit(solution)/shard_map/all_to_all | solution.py:233
  127.2 15.6 %collective-permute-start.2 = (f32[256,256]{1,0:T(8,128)S(1)}, f32[256,256]{1,0:T(8,128)S(1)}, u32[]{:S(2)}, u32[]{:S(2)}) collective-permute-start(f32[256,256]{1,0:T(8,128)S(1)} %bitcast.21), channel_id=1, source_target_pairs={{0,4},{4,0},{1,5},{5,1},{2,6},{6,2},{3,7},{7,3},{8,12},{12,8},{9,1... | collective-permute-start | bytes 786440 | tf_op jit(solution)/shard_map/ppermute | solution.py:242
  135.2 20.3 %all-to-all-start.5 = ((f32[128,1,256]{2,1,0:T(1,128)}), f32[128,1,256]{2,1,0:T(1,128)S(1)}, u32[]{:S(2)}, u32[]{:S(2)}) async-start(f32[128,1,256]{2,1,0:T(1,128)} %copy.9._), calls=%async_computation.5 | async-start | bytes 262144 | tf_op jit(solution)/shard_map/all_to_all | solution.py:233

commit v3 on v2

--- a/solution.py
+++ b/solution.py
@@ -290,7 +290,7 @@
         flops=heavy, waits=1,
     )
 
-    near, far = ("y",) + COL, ("aa", "core")
+    near, far = ("aa", "y"), ("core",) + COL
     raw_c, squares = local_call(apply_kernel, [(1, rank), (axes_size(near), 1, rank)], parts, solve)
     squares = local_call(spread_kernel, [(axes_size(far), 1, rank)], exchange(squares, near))[0]
     scale = functools.partial(scale_kernel, blk_k * n_col)

time: 186 us -> 187 us (level)
  no operation moved by 1% of the time
where the time goes in v3:
time: 187 us; the launch traced here: 186 us
  blocking collectives  88.5 us (47%)
  starting transfers between devices  38.1 us (20%)
  Pallas kernels  34.4 us (18%)
  waiting for transfers between devices  20.9 us (11%)
    all_to_all x4, blocking collectives, exchange(): return lax.all_to_all(blocks, axes, 0, 0, tiled=True)  88.5 us
    pallas_call x10, Pallas kernels, local_call(): pl.pallas_call(kernel, out_shape=[s if isinstance(s, jax.ShapeDtypeStruct...  34.4 us
    all_to_all x4, starting transfers between devices, exchange(): return lax.all_to_all(blocks, axes, 0, 0, tiled=True)  22.5 us
    all_to_all x4, waiting for transfers between devices, exchange(): return lax.all_to_all(blocks, axes, 0, 0, tiled=True)  18.3 us
    ppermute x3, starting transfers between devices, gather_all(): return (own, lax.ppermute(own, 'core', [(0, 1), (1, 0)]))  15.6 us
  transfers between devices with their start and end apart: 7, of which 6 were waited for; matrix products, arithmetic and copies ran while one was open for 1% of the time, Pallas kernels for 15%

profile of v3, /device:TPU:1, one launch (start us, length us, event | category | flops | bytes accessed | tf_op | source)
XLA Modules:
  0.0 186.4 jit_solution(10221285129309381768)
XLA Ops:
  0.6 0.7 pad_maximum_fusion
  1.3 0.3 broadcast_in_dim.10
  1.6 40.5 %all_to_all.40 = f32[256,1,512]{2,1,0:T(1,128)S(1)} all-to-all(f32[256,1,512]{2,1,0:T(1,128)S(1)} %broadcast_in_dim.10), channel_id=1, replica_groups=mesh['aa'=8,'y'=8,'core'=2,'col'=4] {'aa','y','col'}, dimensions={0} | all-to-all | bytes 1048576 | tf_op jit(solution)/shard_map/all_to_all | solution.py:233
  42.1 0.0 copy-start
  42.2 5.2 %collective-permute-start = (f32[256,512]{1,0:T(8,128)S(1)}, f32[256,512]{1,0:T(8,128)S(1)}, u32[]{:S(2)}, u32[]{:S(2)}) collective-permute-start(f32[256,512]{1,0:T(8,128)S(1)} %bitcast.18), channel_id=1, source_target_pairs={{0,4},{4,0},{1,5},{5,1},{2,6},{6,2},{3,7},{7,3},{8,12},{12,8},{9,1... | collective-permute-start | bytes 1572872 | tf_op jit(solution)/shard_map/ppermute | solution.py:242
  47.4 0.1 pad_add_fusion.place_ref
  47.5 1.4 collective-permute-done.other_ref
  48.9 0.0 copy-done
  49.0 2.0 %shard_map.58 = (bf16[128,256]{1,0:T(8,128)(2,1)S(1)}, f32[64,4,256]{2,1,0:T(4,128)}) custom-call(s32[4]{0:T(128)S(1)} %pad_add_fusion.place_ref, bf16[64,32,128]{2,1,0:T(8,128)(2,1)S(1)} %copy-done, f32[256,512]{1,0:T(8,128)S(1)} %bitcast.19, f32[256,512]{1,0:T(8,128)S(1)} %collective-permute-done.other_ref), custom_call_target="tpu_custom_call" | custom-call | flops 4000000000 | bytes 1048576 | tf_op jit(solution)/shard_map/pallas_call | solution.py:215
  50.9 5.5 %all-to-all-start.1 = ((f32[64,4,256]{2,1,0:T(4,128)}), f32[64,4,256]{2,1,0:T(4,128)S(1)}, u32[]{:S(2)}, u32[]{:S(2)}) async-start(f32[64,4,256]{2,1,0:T(4,128)} %get-tuple-element.18._), calls=%async_computation.1 | async-start | bytes 524288 | tf_op jit(solution)/shard_map/all_to_all | solution.py:233
  56.5 9.1 %shard_map.59 = (f32[256,256]{1,0:T(8,128)S(1)}, f32[256,256]{1,0:T(8,128)S(1)}) custom-call(f32[256,512]{1,0:T(8,128)S(1)} %bitcast.20, f32[256,512]{1,0:T(8,128)S(1)} %collective-permute-done.other_ref, f32[64,4,256]{2,1,0:T(4,128)} %get-tuple-element.18._), custom_call_target="tpu_custom_call" | custom-call | flops 12000000000 | bytes 1048576 | tf_op jit(solution)/shard_map/pallas_call | solution.py:215
  65.6 3.1 %all-to-all-done.1.parts_ref = f32[64,4,256]{2,1,0:T(4,128)S(1)} async-done(((f32[64,4,256]{2,1,0:T(4,128)}), f32[64,4,256]{2,1,0:T(4,128)S(1)}, u32[]{:S(2)}, u32[]{:S(2)}) %all-to-all-start.1) | async-done | bytes 262176 | tf_op jit(solution)/shard_map/all_to_all | solution.py:233
  68.7 0.1 shard_map.60
  68.8 18.1 %all_to_all.41 = f32[64,4,256]{2,1,0:T(4,128)S(1)} all-to-all(f32[64,4,256]{2,1,0:T(4,128)S(1)} %shard_map.60), channel_id=1, replica_groups=mesh['aa'=8,'y'=8,'core'=2,'col'=4] {'aa','y'}, dimensions={0} | all-to-all | bytes 524288 | tf_op jit(solution)/shard_map/all_to_all | solution.py:233
  86.9 0.1 reshape.23.own_ref
  87.0 4.9 %collective-permute-start.1 = (f32[256,256]{1,0:T(8,128)S(1)}, f32[256,256]{1,0:T(8,128)S(1)}, u32[]{:S(2)}, u32[]{:S(2)}) collective-permute-start(f32[256,256]{1,0:T(8,128)S(1)} %reshape.23.own_ref), channel_id=1, source_target_pairs={{0,4},{4,0},{1,5},{5,1},{2,6},{6,2},{3,7},{7,3},{8,12},{12,8},{9,1... | collective-permute-start | bytes 786440 | tf_op jit(solution)/shard_map/ppermute | solution.py:242
  91.9 1.1 collective-permute-done.1.other_ref
  93.1 1.9 %shard_map.61 = (f32[64,256]{1,0:T(8,128)S(1)}, f32[1,256]{1,0:T(1,128)S(1)}, f32[32,8,256]{2,1,0:T(8,128)}) custom-call(s32[4]{0:T(128)S(1)} %pad_add_fusion.place_ref, bf16[64,32,128]{2,1,0:T(8,128)(2,1)S(1)} %copy-done, bf16[128,256]{1,0:T(8,128)(2,1)S(1)} %get-tuple-element.21.c_block_ref, f32[256,256]{1,0:T(8,128)S(1)} %reshape.23.own_ref, ...), custom_call_target="tpu_custom_call" | custom-call | flops 4000000000 | bytes 1048576 | tf_op jit(solution)/shard_map/pallas_call | solution.py:215
  95.0 5.6 %all-to-all-start.3 = ((f32[32,8,256]{2,1,0:T(8,128)}), f32[32,8,256]{2,1,0:T(8,128)S(1)}, u32[]{:S(2)}, u32[]{:S(2)}) async-start(f32[32,8,256]{2,1,0:T(8,128)} %get-tuple-element.24._), calls=%async_computation.3 | async-start | bytes 524288 | tf_op jit(solution)/shard_map/all_to_all | solution.py:233
  100.6 9.7 %shard_map.62 = (f32[256,256]{1,0:T(8,128)S(1)}, f32[256,256]{1,0:T(8,128)S(1)}, bf16[64,256]{1,0:T(8,128)(2,1)S(1)}, f32[1,256]{1,0:T(1,128)}) custom-call(f32[256,256]{1,0:T(8,128)S(1)} %reshape.23.own_ref, f32[256,256]{1,0:T(8,128)S(1)} %collective-permute-done.1.other_ref, f32[256,256]{1,0:T(8,128)S(1)} %get-tuple-element.19.refs_0_.solve_ref, ...), custom_call_target="tpu_custom_call" | custom-call | flops 12000000000 | bytes 1048576 | tf_op jit(solution)/shard_map/pallas_call | solution.py:215
  110.3 1.6 all-to-all-done.3.parts_ref
  111.9 0.7 shard_map.63
  112.7 3.9 %all-to-all-start.4 = ((f32[32,8,256]{2,1,0:T(8,128)}), f32[32,8,256]{2,1,0:T(8,128)S(1)}, u32[]{:S(2)}, u32[]{:S(2)}) async-start(f32[32,8,256]{2,1,0:T(8,128)} %shard_map.63), calls=%async_computation.4 | async-start | bytes 524288 | tf_op jit(solution)/shard_map/all_to_all | solution.py:233
  116.6 10.6 %all-to-all-done.4 = f32[32,8,256]{2,1,0:T(8,128)S(1)} async-done(((f32[32,8,256]{2,1,0:T(8,128)}), f32[32,8,256]{2,1,0:T(8,128)S(1)}, u32[]{:S(2)}, u32[]{:S(2)}) %all-to-all-start.4) | async-done | bytes 262176 | tf_op jit(solution)/shard_map/all_to_all | solution.py:233
  127.2 5.5 %collective-permute-start.2 = (f32[256,256]{1,0:T(8,128)S(1)}, f32[256,256]{1,0:T(8,128)S(1)}, u32[]{:S(2)}, u32[]{:S(2)}) collective-permute-start(f32[256,256]{1,0:T(8,128)S(1)} %bitcast.21), channel_id=1, source_target_pairs={{0,4},{4,0},{1,5},{5,1},{2,6},{6,2},{3,7},{7,3},{8,12},{12,8},{9,1... | collective-permute-start | bytes 786440 | tf_op jit(solution)/shard_map/ppermute | solution.py:242
  132.6 0.2 fusion.6.block_ref
  132.9 1.5 fusion
  134.4 0.8 copy.9._
  135.2 7.5 %all-to-all-start.5 = ((f32[128,1,256]{2,1,0:T(1,128)}), f32[128,1,256]{2,1,0:T(1,128)S(1)}, u32[]{:S(2)}, u32[]{:S(2)}) async-start(f32[128,1,256]{2,1,0:T(1,128)} %copy.9._), calls=%async_computation.5 | async-start | bytes 262144 | tf_op jit(solution)/shard_map/all_to_all | solution.py:233
  142.7 0.0 collective-permute-done.2.other_ref
  142.7 9.7 %shard_map.64 = (f32[256,256]{1,0:T(8,128)S(1)}, f32[256,256]{1,0:T(8,128)}, bf16[32,256]{1,0:T(8,128)(2,1)}, f32[1,256]{1,0:T(1,128)}) custom-call(f32[256,256]{1,0:T(8,128)S(1)} %bitcast.23, f32[256,256]{1,0:T(8,128)S(1)} %collective-permute-done.2.other_ref, f32[256,256]{1,0:T(8,128)S(1)} %get-tuple-element.26.refs_0_.solve_ref, ...), custom_call_target="tpu_custom_call" | custom-call | flops 12000000000 | bytes 1048576 | tf_op jit(solution)/shard_map/pallas_call | solution.py:215
  152.5 3.0 %all-to-all-done.5.parts_ref = f32[128,1,256]{2,1,0:T(1,128)S(1)} async-done(((f32[128,1,256]{2,1,0:T(1,128)}), f32[128,1,256]{2,1,0:T(1,128)S(1)}, u32[]{:S(2)}, u32[]{:S(2)}) %all-to-all-start.5) | async-done | bytes 131104 | tf_op jit(solution)/shard_map/all_to_all | solution.py:233
  155.5 0.4 shard_map.65
  155.8 20.7 %all_to_all.42.parts_ref = f32[64,1,256]{2,1,0:T(1,128)S(1)} all-to-all(f32[64,1,256]{2,1,0:T(1,128)S(1)} %get-tuple-element.31), channel_id=1, replica_groups=mesh['aa'=8,'y'=8,'core'=2,'col'=4] {'aa','y'}, dimensions={0} | all-to-all | bytes 131072 | tf_op jit(solution)/shard_map/all_to_all | solution.py:233
  176.5 0.1 shard_map.66
  176.6 9.2 %all_to_all.43.parts_ref = f32[8,1,256]{2,1,0:T(1,128)S(1)} all-to-all(f32[8,1,256]{2,1,0:T(1,128)S(1)} %shard_map.66), channel_id=1, replica_groups=mesh['aa'=8,'y'=8,'core'=2,'col'=4] {'core','col'}, dimensions={0} | all-to-all | bytes 16384 | tf_op jit(solution)/shard_map/all_to_all | solution.py:233
  185.8 0.6 shard_map.67
  (2 shorter events, 0.0 us)
Async XLA Ops:
  42.1 6.8 %copy-start = (bf16[64,32,128]{2,1,0:T(8,128)(2,1)S(1)}, bf16[64,32,128]{2,1,0:T(8,128)(2,1)}, u32[]{:S(2)}) copy-start(bf16[64,32,128]{2,1,0:T(8,128)(2,1)} %tensor_ref.3) | copy-start | bytes 1572868
  42.2 6.8 %collective-permute-start = (f32[256,512]{1,0:T(8,128)S(1)}, f32[256,512]{1,0:T(8,128)S(1)}, u32[]{:S(2)}, u32[]{:S(2)}) collective-permute-start(f32[256,512]{1,0:T(8,128)S(1)} %bitcast.18), channel_id=1, source_target_pairs={{0,4},{4,0},{1,5},{5,1},{2,6},{6,2},{3,7},{7,3},{8,12},{12,8},{9,1... | collective-permute-start | bytes 1572872 | tf_op jit(solution)/shard_map/ppermute | solution.py:242
  50.9 17.8 %all-to-all-start.1 = ((f32[64,4,256]{2,1,0:T(4,128)}), f32[64,4,256]{2,1,0:T(4,128)S(1)}, u32[]{:S(2)}, u32[]{:S(2)}) async-start(f32[64,4,256]{2,1,0:T(4,128)} %get-tuple-element.18._), calls=%async_computation.1 | async-start | bytes 524288 | tf_op jit(solution)/shard_map/all_to_all | solution.py:233
  87.0 6.0 %collective-permute-start.1 = (f32[256,256]{1,0:T(8,128)S(1)}, f32[256,256]{1,0:T(8,128)S(1)}, u32[]{:S(2)}, u32[]{:S(2)}) collective-permute-start(f32[256,256]{1,0:T(8,128)S(1)} %reshape.23.own_ref), channel_id=1, source_target_pairs={{0,4},{4,0},{1,5},{5,1},{2,6},{6,2},{3,7},{7,3},{8,12},{12,8},{9,1... | collective-permute-start | bytes 786440 | tf_op jit(solution)/shard_map/ppermute | solution.py:242
  95.0 16.9 %all-to-all-start.3 = ((f32[32,8,256]{2,1,0:T(8,128)}), f32[32,8,256]{2,1,0:T(8,128)S(1)}, u32[]{:S(2)}, u32[]{:S(2)}) async-start(f32[32,8,256]{2,1,0:T(8,128)} %get-tuple-element.24._), calls=%async_computation.3 | async-start | bytes 524288 | tf_op jit(solution)/shard_map/all_to_all | solution.py:233
  112.7 14.5 %all-to-all-start.4 = ((f32[32,8,256]{2,1,0:T(8,128)}), f32[32,8,256]{2,1,0:T(8,128)S(1)}, u32[]{:S(2)}, u32[]{:S(2)}) async-start(f32[32,8,256]{2,1,0:T(8,128)} %shard_map.63), calls=%async_computation.4 | async-start | bytes 524288 | tf_op jit(solution)/shard_map/all_to_all | solution.py:233
  127.2 15.6 %collective-permute-start.2 = (f32[256,256]{1,0:T(8,128)S(1)}, f32[256,256]{1,0:T(8,128)S(1)}, u32[]{:S(2)}, u32[]{:S(2)}) collective-permute-start(f32[256,256]{1,0:T(8,128)S(1)} %bitcast.21), channel_id=1, source_target_pairs={{0,4},{4,0},{1,5},{5,1},{2,6},{6,2},{3,7},{7,3},{8,12},{12,8},{9,1... | collective-permute-start | bytes 786440 | tf_op jit(solution)/shard_map/ppermute | solution.py:242
  135.2 20.3 %all-to-all-start.5 = ((f32[128,1,256]{2,1,0:T(1,128)}), f32[128,1,256]{2,1,0:T(1,128)S(1)}, u32[]{:S(2)}, u32[]{:S(2)}) async-start(f32[128,1,256]{2,1,0:T(1,128)} %copy.9._), calls=%async_computation.5 | async-start | bytes 262144 | tf_op jit(solution)/shard_map/all_to_all | solution.py:233
